TPU v7x, 128 devices: a whole 4x4x4 slice. The times are simulated.
128 devices in a mesh: src: 32 (over x, z, core), tgt: 4 (over y).
Axes of the slice: x: 4, y: 4, z: 4, core: 2. Of those that a mesh axis runs over, the one named last changes fastest.
Arguments:
- source_embed: bfloat16 [16384, 768], P('src'), may hold values from -16 to 16
- target_embed: bfloat16 [8192, 768], P(('tgt', 'src')), may hold values from -6 to 6
- source_mass: float32 [16384], P('src'), may hold values from 0.3 to 3
- target_mass: float32 [8192], P('tgt'), may hold values from 0.3 to 3
Outputs:
- readout: float32 [16384, 768], P('src')
- source_potential: float32 [16384], P('src')
- target_potential: float32 [8192], P('tgt')
All inputs are finite; a program needn't handle non-finite values.
Results may differ from a plain program's by a relative error of at most 0.0028.
Values may be sent and summed in bfloat16 or wider, within the bound.
A program may use at most 64 MiB of HBM per device.

v0:
```python
import math
import jax
import jax.numpy as jnp
from jax import lax
from jax.sharding import PartitionSpec as P

D = 768
ITERS = 3


def block_scores(sources, block, scale):
    return (
        lax.dot_general(
            sources, block, (((1,), (1,)), ((), ())), preferred_element_type=jnp.float32
        )
        * scale
    )


def row_pass(sources, tgt_blocks, potential_g, scale):
    rows = sources.shape[0]

    def advance(carry, items):
        block, shift = items
        scores = block_scores(sources, block, scale) + shift[None, :]
        peak = jnp.maximum(carry[0], jnp.max(scores, axis=1))
        total = carry[1] * jnp.exp(carry[0] - peak) + jnp.sum(
            jnp.exp(scores - peak[:, None]), axis=1
        )
        return ((peak, total), None)

    start = (jnp.full((rows,), -1e30, jnp.float32), jnp.zeros((rows,), jnp.float32))
    return lax.scan(advance, start, (tgt_blocks, potential_g))[0]


def column_pass(sources, tgt_blocks, potential_f, scale):

    def single(block):
        scores = block_scores(sources, block, scale) + potential_f[:, None]
        peak = jnp.max(scores, axis=0)
        return (peak, jnp.sum(jnp.exp(scores - peak[None, :]), axis=0))

    return lax.map(single, tgt_blocks)


def shards(source_embed, target_embed, source_mass, target_mass):
    scale = 2.0 / math.sqrt(D)
    gathered = lax.all_gather(target_embed, "src", axis=0, tiled=True)
    total_rows = gathered.shape[0]
    width = 512
    count = total_rows // width
    tgt_blocks = gathered.reshape(count, width, gathered.shape[1])
    log_a = jnp.log(source_mass)
    log_b = jnp.log(target_mass).reshape(count, width)
    potential_g = jnp.zeros((count, width), jnp.float32)
    potential_f = jnp.zeros(log_a.shape, jnp.float32)
    for step in range(ITERS):
        peak, total = row_pass(source_embed, tgt_blocks, potential_g, scale)
        highest = lax.pmax(peak, "tgt")
        total = lax.psum(total * jnp.exp(peak - highest), "tgt")
        peak = highest
        potential_f = log_a - (peak + jnp.log(total))
        column_peak, column_total = column_pass(source_embed, tgt_blocks, potential_f, scale)
        column_high = lax.pmax(column_peak, "src")
        column_total = lax.psum(column_total * jnp.exp(column_peak - column_high), "src")
        column_peak = column_high
        potential_g = log_b - (column_peak + jnp.log(column_total))
    offset = potential_f - log_a

    def gather_step(carry, items):
        block, shift = items
        weights = jnp.exp(
            block_scores(source_embed, block, scale) + shift[None, :] + offset[:, None]
        )
        numer = carry[0] + jnp.dot(
            weights.astype(jnp.bfloat16), block, preferred_element_type=jnp.float32
        )
        return ((numer, carry[1] + jnp.sum(weights, axis=1)), None)

    rows = source_embed.shape[0]
    start = (jnp.zeros((rows, gathered.shape[1]), jnp.float32), jnp.zeros((rows,), jnp.float32))
    numerator, mass = lax.scan(gather_step, start, (tgt_blocks, potential_g))[0]
    numerator, mass = lax.psum((numerator, mass), "tgt")
    readout = numerator / mass[:, None]
    return (readout, potential_f, potential_g.reshape(total_rows))


def solution(mesh):
    placed = (P("src", None), P(("tgt", "src"), None), P("src"), P("tgt"))
    return jax.shard_map(
        shards,
        mesh=mesh,
        in_specs=placed,
        out_specs=(P("src", None), P("src"), P("tgt")),
        check_vma=False,
    )
```

profile of v0, /device:TPU:1, one launch (start us, length us, event | category | flops | bytes accessed | tf_op | source)
XLA Modules:
  0.0 622.1 jit_solution(17024977472537300388)
XLA Ops:
  8.7 50.4 %all-gather.2.cloned.1.call-done = bf16[2048,768]{1,0:T(8,128)(2,1)} async-done(((bf16[64,768]{1,0:T(8,128)(2,1)}), bf16[2048,768]{1,0:T(8,128)(2,1)}) %all-gather.2.cloned.1.call-update) | async-done | bytes 3145744 | tf_op jit(solution)/shard_map/all_gather | solution.py:48
  59.1 9.0 %while.91 = (s32[]{:T(128)}, f32[512]{0:T(512)S(1)}, f32[512]{0:T(512)S(1)}, bf16[4,512,768]{2,1,0:T(8,128)(2,1)}, bf16[512,768]{1,0:T(8,128)(2,1)}, /*index=5*/s32[]{:T(128)}, s32[]{:T(128)}) while((s32[]{:T(128)}, f32[512]{0:T(512)S(1)}, f32[512]{0:T(512)S(1)}, bf16[4,512,768]{2,1,0:T(8,128)(2,1)}, bf16[512,768]{1,0:T(8,128)(2,1)}, ...), condition=%wide.region_3.4_spmd.clone, body=%wide.region_0.3_spmd.clone.sunk | while | flops 403704320 | bytes 3697240 | solution.py:33
  59.1 2.0 fusion.77
  68.1 8.5 %pmax.42 = f32[512]{0:T(512)S(1)} all-reduce(f32[512]{0:T(512)S(1)} %get-tuple-element.234), channel_id=1, replica_groups=mesh['src'=32,'tgt'=4] {'tgt'}, use_global_device_ids=true, to_apply=%region_4.5 | all-reduce | flops 512 | bytes 4096 | tf_op jit(solution)/shard_map/pmax | solution.py:59
  76.5 6.0 psum.56
  82.6 9.2 %while.88 = (s32[]{:T(128)}, f32[4,512]{1,0:T(4,128)S(1)}, f32[4,512]{1,0:T(4,128)S(1)}, bf16[4,512,768]{2,1,0:T(8,128)(2,1)}, bf16[512,768]{1,0:T(8,128)(2,1)}, /*index=5*/f32[512]{0:T(512)S(1)}, s32[]{:T(128)}, s32[]{:T(128)}) while((s32[]{:T(128)}, f32[4,512]{1,0:T(4,128)S(1)}, f32[4,512]{1,0:T(4,128)S(1)}, ...), condition=%wide.region_9.10_spmd, body=%wide.region_6.9_spmd.sunk | while | flops 403962880 | bytes 3687005 | solution.py:43
  91.8 67.0 %pmax.43 = f32[4,512]{1,0:T(4,128)S(1)} all-reduce(f32[4,512]{1,0:T(4,128)S(1)} %get-tuple-element.236), channel_id=1, replica_groups=mesh['src'=32,'tgt'=4] {'src'}, use_global_device_ids=true, to_apply=%region_10.11 | all-reduce | flops 2048 | bytes 16384 | tf_op jit(solution)/shard_map/pmax | solution.py:64
  158.8 63.7 %psum.57 = f32[4,512]{1,0:T(4,128)S(1)} all-reduce(f32[4,512]{1,0:T(4,128)S(1)} %exponential_multiply_fusion.2), channel_id=1, replica_groups=mesh['src'=32,'tgt'=4] {'src'}, use_global_device_ids=true, to_apply=%region_11.12 | all-reduce | flops 2048 | bytes 16384 | tf_op jit(solution)/shard_map/psum | solution.py:65
  222.6 9.0 %while.92 = (s32[]{:T(128)}, f32[512]{0:T(512)S(1)}, f32[512]{0:T(512)S(1)}, bf16[4,512,768]{2,1,0:T(8,128)(2,1)}, bf16[512,768]{1,0:T(8,128)(2,1)}, /*index=5*/f32[4,512]{1,0:T(4,128)S(1)}, s32[]{:T(128)}, s32[]{:T(128)}) while((s32[]{:T(128)}, f32[512]{0:T(512)S(1)}, f32[512]{0:T(512)S(1)}, bf16[4,512,768]{2,1,0:T(8,128)(2,1)}, ...), condition=%wide.region_15.16_spmd.clone, body=%wide.region_12.15_spmd.clone.sunk | while | flops 403966464 | bytes 3703396 | solution.py:33
  231.6 7.7 %pmax.44 = f32[512]{0:T(512)S(1)} all-reduce(f32[512]{0:T(512)S(1)} %get-tuple-element.238), channel_id=1, replica_groups=mesh['src'=32,'tgt'=4] {'tgt'}, use_global_device_ids=true, to_apply=%region_16.17 | all-reduce | flops 512 | bytes 4096 | tf_op jit(solution)/shard_map/pmax | solution.py:59
  239.3 6.0 psum.58
  245.4 9.2 %while.89 = (s32[]{:T(128)}, f32[4,512]{1,0:T(4,128)S(1)}, f32[4,512]{1,0:T(4,128)S(1)}, bf16[4,512,768]{2,1,0:T(8,128)(2,1)}, bf16[512,768]{1,0:T(8,128)(2,1)}, /*index=5*/f32[512]{0:T(512)S(1)}, s32[]{:T(128)}, s32[]{:T(128)}) while((s32[]{:T(128)}, f32[4,512]{1,0:T(4,128)S(1)}, f32[4,512]{1,0:T(4,128)S(1)}, ...), condition=%wide.region_21.22_spmd, body=%wide.region_18.21_spmd.sunk | while | flops 403962880 | bytes 3687005 | solution.py:43
  254.6 67.4 %pmax.45 = f32[4,512]{1,0:T(4,128)S(1)} all-reduce(f32[4,512]{1,0:T(4,128)S(1)} %get-tuple-element.240), channel_id=1, replica_groups=mesh['src'=32,'tgt'=4] {'src'}, use_global_device_ids=true, to_apply=%region_22.23 | all-reduce | flops 2048 | bytes 16384 | tf_op jit(solution)/shard_map/pmax | solution.py:64
  322.1 63.7 %psum.59 = f32[4,512]{1,0:T(4,128)S(1)} all-reduce(f32[4,512]{1,0:T(4,128)S(1)} %exponential_multiply_fusion.1), channel_id=1, replica_groups=mesh['src'=32,'tgt'=4] {'src'}, use_global_device_ids=true, to_apply=%region_23.24 | all-reduce | flops 2048 | bytes 16384 | tf_op jit(solution)/shard_map/psum | solution.py:65
  385.8 9.0 %while.93 = (s32[]{:T(128)}, f32[512]{0:T(512)S(1)}, f32[512]{0:T(512)S(1)}, bf16[4,512,768]{2,1,0:T(8,128)(2,1)}, bf16[512,768]{1,0:T(8,128)(2,1)}, /*index=5*/f32[4,512]{1,0:T(4,128)S(1)}, s32[]{:T(128)}, s32[]{:T(128)}) while((s32[]{:T(128)}, f32[512]{0:T(512)S(1)}, f32[512]{0:T(512)S(1)}, bf16[4,512,768]{2,1,0:T(8,128)(2,1)}, ...), condition=%wide.region_27.28_spmd.clone, body=%wide.region_24.27_spmd.clone.sunk | while | flops 403966464 | bytes 3703396 | solution.py:33
  394.8 7.7 %pmax.46 = f32[512]{0:T(512)S(1)} all-reduce(f32[512]{0:T(512)S(1)} %get-tuple-element.242), channel_id=1, replica_groups=mesh['src'=32,'tgt'=4] {'tgt'}, use_global_device_ids=true, to_apply=%region_28.29 | all-reduce | flops 512 | bytes 4096 | tf_op jit(solution)/shard_map/pmax | solution.py:59
  402.6 6.0 psum.60
  408.6 9.2 %while.90 = (s32[]{:T(128)}, f32[4,512]{1,0:T(4,128)S(1)}, f32[4,512]{1,0:T(4,128)S(1)}, bf16[4,512,768]{2,1,0:T(8,128)(2,1)}, bf16[512,768]{1,0:T(8,128)(2,1)}, /*index=5*/f32[512]{0:T(512)S(1)}, s32[]{:T(128)}, s32[]{:T(128)}) while((s32[]{:T(128)}, f32[4,512]{1,0:T(4,128)S(1)}, f32[4,512]{1,0:T(4,128)S(1)}, ...), condition=%wide.region_33.34_spmd, body=%wide.region_30.33_spmd.sunk | while | flops 403962880 | bytes 3687005 | solution.py:43
  417.9 67.4 %pmax.47 = f32[4,512]{1,0:T(4,128)S(1)} all-reduce(f32[4,512]{1,0:T(4,128)S(1)} %get-tuple-element.244), channel_id=1, replica_groups=mesh['src'=32,'tgt'=4] {'src'}, use_global_device_ids=true, to_apply=%region_34.35 | all-reduce | flops 2048 | bytes 16384 | tf_op jit(solution)/shard_map/pmax | solution.py:64
  485.3 63.7 %psum.61 = f32[4,512]{1,0:T(4,128)S(1)} all-reduce(f32[4,512]{1,0:T(4,128)S(1)} %exponential_multiply_fusion), channel_id=1, replica_groups=mesh['src'=32,'tgt'=4] {'src'}, use_global_device_ids=true, to_apply=%region_35.36 | all-reduce | flops 2048 | bytes 16384 | tf_op jit(solution)/shard_map/psum | solution.py:65
  549.1 16.6 %while.94 = (s32[]{:T(128)}, f32[512,768]{1,0:T(8,128)S(1)}, f32[512]{0:T(512)S(1)}, bf16[4,512,768]{2,1,0:T(8,128)(2,1)}, bf16[512,768]{1,0:T(8,128)(2,1)}, /*i...) while((s32[]{:T(128)}, f32[512,768]{1,0:T(8,128)S(1)}, f32[512]{0:T(512)S(1)}, ...), condition=%wide.region_38.39_spmd.clone, body=%wide.region_36.38_spmd.clone.sunk | while | flops 807404032 | bytes 6571116 | solution.py:82
  549.1 2.1 fusion.88
  551.2 2.0 select_add_fusion.4
  553.2 2.1 fusion.88
  555.3 2.0 select_add_fusion.4
  557.4 2.1 fusion.88
  559.5 2.0 select_add_fusion.4
  561.5 2.1 fusion.88
  563.6 2.0 select_add_fusion.4
  567.4 8.6 %psum.63 = f32[512]{0:T(512)S(1)} all-reduce(f32[512]{0:T(512)S(1)} %get-tuple-element.247), channel_id=1, replica_groups=mesh['src'=32,'tgt'=4] {'tgt'}, use_global_device_ids=true, to_apply=%region_40.41 | all-reduce | flops 512 | bytes 4096 | tf_op jit(solution)/shard_map/psum | solution.py:83
  576.0 36.6 %all-reduce.2.cloned.1.call-done = f32[512,768]{1,0:T(8,128)} async-done(((f32[512,768]{1,0:T(8,128)}), f32[512,768]{1,0:T(8,128)}) %all-reduce.2.cloned.1.call-update) | async-done | bytes 1572880 | tf_op jit(solution)/shard_map/psum | solution.py:83
  612.6 2.7 broadcast_divide_fusion
  (162 shorter events, 55.5 us)
Async XLA Ops:
  7.2 51.9 %all-gather.2.cloned.1.call-start = ((), (), s32[]{:S(2)}) async-start(), calls=%async_computation | async-start | bytes 3244032 | tf_op jit(solution)/shard_map/all_gather | solution.py:48
  7.9 604.7 %all-reduce.2.cloned.1.call-start = ((), (), s32[]{:S(2)}) async-start(), calls=%async_computation.1 | async-start | bytes 3145728 | tf_op jit(solution)/shard_map/psum | solution.py:83
  59.1 23.4 %copy-start.1 = (f32[512]{0:T(512)S(1)}, f32[512]{0:T(512)}, u32[]{:S(2)}) copy-start(f32[512]{0:T(512)} %param.20) | copy-start | bytes 6148
  417.9 131.2 %copy-start.2 = (f32[512]{0:T(512)}, f32[512]{0:T(512)S(1)}, u32[]{:S(2)}) copy-start(f32[512]{0:T(512)S(1)} %get-tuple-element.904) | copy-start | bytes 6148
  565.6 1.1 copy-start
Sparse Core Ops, SparseCore 0:
  10.3 48.8 all-gather.1
  566.9 45.5 all-reduce.1
where the time goes:
time: 623 us; the launch traced here: 622 us
  blocking collectives  443 us (71%)
  waiting for transfers between devices  87.7 us (14%)
  matrix products  64.1 us (10%)
  between operations  14.3 us (2%)
  other arithmetic  7.88 us (1%)
    pmax x3, blocking collectives, shards(): column_high = lax.pmax(column_peak, 'src')  202 us
    psum x3, blocking collectives, shards(): lax.psum(column_total * jnp.exp(column_peak - column_high), 'src')  191 us
    dot_general x28, matrix products, block_scores(): lax.dot_general(sources, block, (((1,), (1,)), ((), ())), preferred_eleme...  56.1 us
    all_gather x1, waiting for transfers between devices, shards(): gathered = lax.all_gather(target_embed, 'src', axis=0, tiled=True)  50.4 us
    psum x1, waiting for transfers between devices, shards(): numerator, mass = lax.psum((numerator, mass), 'tgt')  36.6 us
    pmax x3, blocking collectives, shards(): highest = lax.pmax(peak, 'tgt')  23.9 us
    psum x3, blocking collectives, shards(): total = lax.psum(total * jnp.exp(peak - highest), 'tgt')  18 us
  transfers between devices with their start and end apart: 2, of which 2 were waited for; matrix products, arithmetic and copies ran while one was open for 0% of the time, Pallas kernels for 0%

commit v1 on v0

--- a/solution.py
+++ b/solution.py
@@ -62,7 +62,9 @@
         potential_f = log_a - (peak + jnp.log(total))
         column_peak, column_total = column_pass(source_embed, tgt_blocks, potential_f, scale)
         column_high = lax.pmax(column_peak, "src")
-        column_total = lax.psum(column_total * jnp.exp(column_peak - column_high), "src")
+        own = column_total * jnp.exp(column_peak - column_high)
+        parts = lax.all_gather(own, "src", axis=0, tiled=False)
+        column_total = parts.sum(axis=0)
         column_peak = column_high
         potential_g = log_b - (column_peak + jnp.log(column_total))
     offset = potential_f - log_a

time: 623 us -> 502 us (0.81)
  blocking collectives: 443 us -> 318 us
    psum x3 -> x0, blocking collectives: 191 us -> none  [shards(): lax.psum(column_total * jnp.exp(column_peak - column_high), 'src')]
    all_gather x0 -> x3, blocking collectives: none -> 67.1 us  [shards(): parts = lax.all_gather(own, 'src', axis=0, tiled=False)]
where the time goes in v1:
time: 502 us; the launch traced here: 500 us
  blocking collectives  318 us (63%)
  waiting for transfers between devices  91.5 us (18%)
  matrix products  64.1 us (13%)
  between operations  14.3 us (3%)
  other arithmetic  8.07 us (2%)
    pmax x3, blocking collectives, shards(): column_high = lax.pmax(column_peak, 'src')  201 us
    all_gather x3, blocking collectives, shards(): parts = lax.all_gather(own, 'src', axis=0, tiled=False)  67.1 us
    dot_general x28, matrix products, block_scores(): lax.dot_general(sources, block, (((1,), (1,)), ((), ())), preferred_eleme...  56.1 us
    all_gather x1, waiting for transfers between devices, shards(): gathered = lax.all_gather(target_embed, 'src', axis=0, tiled=True)  50.4 us
    psum x1, waiting for transfers between devices, shards(): numerator, mass = lax.psum((numerator, mass), 'tgt')  40.4 us
    pmax x3, blocking collectives, shards(): highest = lax.pmax(peak, 'tgt')  23.9 us
    psum x3, blocking collectives, shards(): total = lax.psum(total * jnp.exp(peak - highest), 'tgt')  18 us
  transfers between devices with their start and end apart: 2, of which 2 were waited for; matrix products, arithmetic and copies ran while one was open for 0% of the time, Pallas kernels for 0%

profile of v1, /device:TPU:1, one launch (start us, length us, event | category | flops | bytes accessed | tf_op | source)
XLA Modules:
  0.0 500.2 jit_solution(6522222362852981781)
XLA Ops:
  8.7 50.4 %all-gather.8.cloned.1.call-done = bf16[2048,768]{1,0:T(8,128)(2,1)} async-done(((bf16[64,768]{1,0:T(8,128)(2,1)}), bf16[2048,768]{1,0:T(8,128)(2,1)}) %all-gather.8.cloned.1.call-update) | async-done | bytes 3145744 | tf_op jit(solution)/shard_map/all_gather | solution.py:48
  59.1 9.0 %while.91 = (s32[]{:T(128)}, f32[512]{0:T(512)S(1)}, f32[512]{0:T(512)S(1)}, bf16[4,512,768]{2,1,0:T(8,128)(2,1)}, bf16[512,768]{1,0:T(8,128)(2,1)}, /*index=5*/s32[]{:T(128)}, s32[]{:T(128)}) while((s32[]{:T(128)}, f32[512]{0:T(512)S(1)}, f32[512]{0:T(512)S(1)}, bf16[4,512,768]{2,1,0:T(8,128)(2,1)}, bf16[512,768]{1,0:T(8,128)(2,1)}, ...), condition=%wide.region_3.4_spmd.clone, body=%wide.region_0.3_spmd.clone.sunk | while | flops 403704320 | bytes 3697240 | solution.py:33
  59.1 2.0 fusion.77
  68.1 8.5 %pmax.42 = f32[512]{0:T(512)S(1)} all-reduce(f32[512]{0:T(512)S(1)} %get-tuple-element.234), channel_id=1, replica_groups=mesh['src'=32,'tgt'=4] {'tgt'}, use_global_device_ids=true, to_apply=%region_4.5 | all-reduce | flops 512 | bytes 4096 | tf_op jit(solution)/shard_map/pmax | solution.py:59
  76.5 6.0 %psum.35 = f32[512]{0:T(512)S(1)} all-reduce(f32[512]{0:T(512)S(1)} %exponential_multiply_fusion.2), channel_id=1, replica_groups=mesh['src'=32,'tgt'=4] {'tgt'}, use_global_device_ids=true, to_apply=%region_5.6 | all-reduce | flops 512 | bytes 4096 | tf_op jit(solution)/shard_map/psum | solution.py:60
  82.6 9.2 %while.88 = (s32[]{:T(128)}, f32[4,512]{1,0:T(4,128)S(1)}, f32[4,512]{1,0:T(4,128)S(1)}, bf16[4,512,768]{2,1,0:T(8,128)(2,1)}, bf16[512,768]{1,0:T(8,128)(2,1)}, /*index=5*/f32[512]{0:T(512)S(1)}, s32[]{:T(128)}, s32[]{:T(128)}) while((s32[]{:T(128)}, f32[4,512]{1,0:T(4,128)S(1)}, f32[4,512]{1,0:T(4,128)S(1)}, ...), condition=%wide.region_9.10_spmd, body=%wide.region_6.9_spmd.sunk | while | flops 403962880 | bytes 3687005 | solution.py:43
  91.8 67.0 %pmax.43 = f32[4,512]{1,0:T(4,128)S(1)} all-reduce(f32[4,512]{1,0:T(4,128)S(1)} %get-tuple-element.236), channel_id=1, replica_groups=mesh['src'=32,'tgt'=4] {'src'}, use_global_device_ids=true, to_apply=%region_10.11 | all-reduce | flops 2048 | bytes 16384 | tf_op jit(solution)/shard_map/pmax | solution.py:64
  158.8 22.4 %all-gather.3 = f32[32,4,512]{2,1,0:T(4,128)S(1)} all-gather(f32[1,4,512]{2,1,0:T(4,128)S(1)} %multiply_bitcast_fusion.2), channel_id=2, replica_groups=mesh['src'=32,'tgt'=4] {'src'}, dimensions={0}, use_global_device_ids=true | all-gather | bytes 270336 | tf_op jit(solution)/shard_map/all_gather | solution.py:66
  181.3 9.0 %while.92 = (s32[]{:T(128)}, f32[512]{0:T(512)S(1)}, f32[512]{0:T(512)S(1)}, bf16[4,512,768]{2,1,0:T(8,128)(2,1)}, bf16[512,768]{1,0:T(8,128)(2,1)}, /*index=5*/f32[4,512]{1,0:T(4,128)S(1)}, s32[]{:T(128)}, s32[]{:T(128)}) while((s32[]{:T(128)}, f32[512]{0:T(512)S(1)}, f32[512]{0:T(512)S(1)}, bf16[4,512,768]{2,1,0:T(8,128)(2,1)}, ...), condition=%wide.region_15.16_spmd.clone, body=%wide.region_12.15_spmd.clone.sunk | while | flops 403966464 | bytes 3703396 | solution.py:33
  190.3 7.7 %pmax.44 = f32[512]{0:T(512)S(1)} all-reduce(f32[512]{0:T(512)S(1)} %get-tuple-element.238), channel_id=1, replica_groups=mesh['src'=32,'tgt'=4] {'tgt'}, use_global_device_ids=true, to_apply=%region_16.17 | all-reduce | flops 512 | bytes 4096 | tf_op jit(solution)/shard_map/pmax | solution.py:59
  198.1 6.0 %psum.36 = f32[512]{0:T(512)S(1)} all-reduce(f32[512]{0:T(512)S(1)} %exponential_multiply_fusion.1), channel_id=1, replica_groups=mesh['src'=32,'tgt'=4] {'tgt'}, use_global_device_ids=true, to_apply=%region_17.18 | all-reduce | flops 512 | bytes 4096 | tf_op jit(solution)/shard_map/psum | solution.py:60
  204.1 9.2 %while.89 = (s32[]{:T(128)}, f32[4,512]{1,0:T(4,128)S(1)}, f32[4,512]{1,0:T(4,128)S(1)}, bf16[4,512,768]{2,1,0:T(8,128)(2,1)}, bf16[512,768]{1,0:T(8,128)(2,1)}, /*index=5*/f32[512]{0:T(512)S(1)}, s32[]{:T(128)}, s32[]{:T(128)}) while((s32[]{:T(128)}, f32[4,512]{1,0:T(4,128)S(1)}, f32[4,512]{1,0:T(4,128)S(1)}, ...), condition=%wide.region_21.22_spmd, body=%wide.region_18.21_spmd.sunk | while | flops 403962880 | bytes 3687005 | solution.py:43
  213.3 66.9 %pmax.45 = f32[4,512]{1,0:T(4,128)S(1)} all-reduce(f32[4,512]{1,0:T(4,128)S(1)} %get-tuple-element.240), channel_id=1, replica_groups=mesh['src'=32,'tgt'=4] {'src'}, use_global_device_ids=true, to_apply=%region_22.23 | all-reduce | flops 2048 | bytes 16384 | tf_op jit(solution)/shard_map/pmax | solution.py:64
  280.3 22.4 %all-gather.4 = f32[32,4,512]{2,1,0:T(4,128)S(1)} all-gather(f32[1,4,512]{2,1,0:T(4,128)S(1)} %multiply_bitcast_fusion.1), channel_id=3, replica_groups=mesh['src'=32,'tgt'=4] {'src'}, dimensions={0}, use_global_device_ids=true | all-gather | bytes 270336 | tf_op jit(solution)/shard_map/all_gather | solution.py:66
  302.7 9.0 %while.93 = (s32[]{:T(128)}, f32[512]{0:T(512)S(1)}, f32[512]{0:T(512)S(1)}, bf16[4,512,768]{2,1,0:T(8,128)(2,1)}, bf16[512,768]{1,0:T(8,128)(2,1)}, /*index=5*/f32[4,512]{1,0:T(4,128)S(1)}, s32[]{:T(128)}, s32[]{:T(128)}) while((s32[]{:T(128)}, f32[512]{0:T(512)S(1)}, f32[512]{0:T(512)S(1)}, bf16[4,512,768]{2,1,0:T(8,128)(2,1)}, ...), condition=%wide.region_27.28_spmd.clone, body=%wide.region_24.27_spmd.clone.sunk | while | flops 403966464 | bytes 3703396 | solution.py:33
  311.8 7.7 %pmax.46 = f32[512]{0:T(512)S(1)} all-reduce(f32[512]{0:T(512)S(1)} %get-tuple-element.242), channel_id=1, replica_groups=mesh['src'=32,'tgt'=4] {'tgt'}, use_global_device_ids=true, to_apply=%region_28.29 | all-reduce | flops 512 | bytes 4096 | tf_op jit(solution)/shard_map/pmax | solution.py:59
  319.5 6.0 %psum.37 = f32[512]{0:T(512)S(1)} all-reduce(f32[512]{0:T(512)S(1)} %exponential_multiply_fusion), channel_id=1, replica_groups=mesh['src'=32,'tgt'=4] {'tgt'}, use_global_device_ids=true, to_apply=%region_29.30 | all-reduce | flops 512 | bytes 4096 | tf_op jit(solution)/shard_map/psum | solution.py:60
  325.5 9.2 %while.90 = (s32[]{:T(128)}, f32[4,512]{1,0:T(4,128)S(1)}, f32[4,512]{1,0:T(4,128)S(1)}, bf16[4,512,768]{2,1,0:T(8,128)(2,1)}, bf16[512,768]{1,0:T(8,128)(2,1)}, /*index=5*/f32[512]{0:T(512)S(1)}, s32[]{:T(128)}, s32[]{:T(128)}) while((s32[]{:T(128)}, f32[4,512]{1,0:T(4,128)S(1)}, f32[4,512]{1,0:T(4,128)S(1)}, ...), condition=%wide.region_33.34_spmd, body=%wide.region_30.33_spmd.sunk | while | flops 403962880 | bytes 3687005 | solution.py:43
  334.8 66.9 %pmax.47 = f32[4,512]{1,0:T(4,128)S(1)} all-reduce(f32[4,512]{1,0:T(4,128)S(1)} %get-tuple-element.244), channel_id=1, replica_groups=mesh['src'=32,'tgt'=4] {'src'}, use_global_device_ids=true, to_apply=%region_34.35 | all-reduce | flops 2048 | bytes 16384 | tf_op jit(solution)/shard_map/pmax | solution.py:64
  401.7 22.4 %all-gather.5 = f32[32,4,512]{2,1,0:T(4,128)S(1)} all-gather(f32[1,4,512]{2,1,0:T(4,128)S(1)} %multiply_bitcast_fusion), channel_id=4, replica_groups=mesh['src'=32,'tgt'=4] {'src'}, dimensions={0}, use_global_device_ids=true | all-gather | bytes 270336 | tf_op jit(solution)/shard_map/all_gather | solution.py:66
  424.2 16.6 %while.94 = (s32[]{:T(128)}, f32[512,768]{1,0:T(8,128)S(1)}, f32[512]{0:T(512)S(1)}, bf16[4,512,768]{2,1,0:T(8,128)(2,1)}, bf16[512,768]{1,0:T(8,128)(2,1)}, /*i...) while((s32[]{:T(128)}, f32[512,768]{1,0:T(8,128)S(1)}, f32[512]{0:T(512)S(1)}, ...), condition=%wide.region_38.39_spmd.clone, body=%wide.region_36.38_spmd.clone.sunk | while | flops 807404032 | bytes 6571116 | solution.py:84
  424.2 2.1 fusion.88
  426.3 2.0 select_add_fusion.4
  428.4 2.1 fusion.88
  430.5 2.0 select_add_fusion.4
  432.5 2.1 fusion.88
  434.6 2.0 select_add_fusion.4
  436.7 2.1 fusion.88
  438.7 2.0 select_add_fusion.4
  442.5 7.7 %psum.39 = f32[512]{0:T(512)S(1)} all-reduce(f32[512]{0:T(512)S(1)} %get-tuple-element.247), channel_id=1, replica_groups=mesh['src'=32,'tgt'=4] {'tgt'}, use_global_device_ids=true, to_apply=%region_40.41 | all-reduce | flops 512 | bytes 4096 | tf_op jit(solution)/shard_map/psum | solution.py:85
  450.2 40.4 %all-reduce.2.cloned.1.call-done = f32[512,768]{1,0:T(8,128)} async-done(((f32[512,768]{1,0:T(8,128)}), f32[512,768]{1,0:T(8,128)}) %all-reduce.2.cloned.1.call-update) | async-done | bytes 1572880 | tf_op jit(solution)/shard_map/psum | solution.py:85
  490.7 2.7 broadcast_divide_fusion
  (165 shorter events, 55.6 us)
Async XLA Ops:
  7.2 51.9 %all-gather.8.cloned.1.call-start = ((), (), s32[]{:S(2)}) async-start(), calls=%async_computation | async-start | bytes 3244032 | tf_op jit(solution)/shard_map/all_gather | solution.py:48
  7.9 482.8 %all-reduce.2.cloned.1.call-start = ((), (), s32[]{:S(2)}) async-start(), calls=%async_computation.1 | async-start | bytes 3145728 | tf_op jit(solution)/shard_map/psum | solution.py:85
  59.1 23.4 %copy-start.1 = (f32[512]{0:T(512)S(1)}, f32[512]{0:T(512)}, u32[]{:S(2)}) copy-start(f32[512]{0:T(512)} %param.20) | copy-start | bytes 6148
  334.8 89.4 %copy-start.2 = (f32[512]{0:T(512)}, f32[512]{0:T(512)S(1)}, u32[]{:S(2)}) copy-start(f32[512]{0:T(512)S(1)} %get-tuple-element.904) | copy-start | bytes 6148
  440.8 1.1 copy-start
Sparse Core Ops, SparseCore 0:
  10.3 48.8 all-gather.7
  442.1 48.5 all-reduce.1
